TPU v7x, 256 devices: a whole 4x4x8 slice. The times are simulated.
256 devices in a mesh: view: 8 (over z), wide: 32 (over y, x, core).
Axes of the slice: x: 4, y: 4, z: 8, core: 2. Of those that a mesh axis runs over, the one named last changes fastest.
Arguments:
- tracer: float32 [512, 1024, 128], P('view', 'wide'), may hold values from 0.05 to 5
- velocity: float32 [3, 512, 1024, 128], P(None, 'view', 'wide'), may hold values from -0.15 to 0.15
- buildings: int32 [512, 1024, 128], P('view', 'wide'), may hold values from 0 to 1, as said below
- source: float32 [512, 1024, 128], P('view', 'wide'), may hold values from 0 to 0.5
Outputs:
- tracer_next: float32 [512, 1024, 128], P('view', 'wide')
- picture: float32 [4, 1024, 128], P(None, 'wide', 'view')
Inputs may be any that keep to these rules, and one draw needn't show every extreme that they name: `buildings`: each column of cells at a fixed first and second index is inside a building from the ground up to some height of at most 64 cells, and outside above it.
All inputs are finite; a program needn't handle non-finite values.
Results may differ from a plain program's by a relative error of at most 0.000056.
Values sent between devices are 32-bit elements; how exact they have to be, the bound alone decides.
A program may use at most 64 MiB of HBM per device.

v0:
```python
import jax
import jax.numpy as jnp
from jax import lax
from jax.sharding import PartitionSpec as P

STEPS = 4


def padded_2(cells, sides, width):
    for axis, dim in sides:
        count = lax.axis_size(axis)
        head = lax.slice_in_dim(cells, 0, width, axis=dim)
        tail = lax.slice_in_dim(cells, cells.shape[dim] - width, cells.shape[dim], axis=dim)
        cells = jnp.concatenate(
            [
                lax.ppermute(tail, axis, [(i, (i + 1) % count) for i in range(count)]),
                cells,
                lax.ppermute(head, axis, [((i + 1) % count, i) for i in range(count)]),
            ],
            axis=dim,
        )
    return cells


def advance(tracer, velocity, open_cells, source):
    face_zero = velocity[0][:-1] * open_cells[:-1] * open_cells[1:]
    flux_zero = jnp.maximum(face_zero, 0.0) * tracer[:-1] + jnp.minimum(face_zero, 0.0) * tracer[1:]
    delta_zero = (flux_zero[1:] - flux_zero[:-1])[:, 1:-1]
    face_one = velocity[1][:, :-1] * open_cells[:, :-1] * open_cells[:, 1:]
    flux_one = (
        jnp.maximum(face_one, 0.0) * tracer[:, :-1] + jnp.minimum(face_one, 0.0) * tracer[:, 1:]
    )
    delta_one = (flux_one[:, 1:] - flux_one[:, :-1])[1:-1]
    face_two = velocity[2][:, :, :-1] * open_cells[:, :, :-1] * open_cells[:, :, 1:]
    flux_two = (
        jnp.maximum(face_two, 0.0) * tracer[:, :, :-1]
        + jnp.minimum(face_two, 0.0) * tracer[:, :, 1:]
    )
    padded = jnp.pad(flux_two, ((0, 0), (0, 0), (1, 1)))
    delta_two = (padded[:, :, 1:] - padded[:, :, :-1])[1:-1, 1:-1]
    inner_tracer = tracer[1:-1, 1:-1]
    return open_cells[1:-1, 1:-1] * (
        inner_tracer - delta_zero - delta_one - delta_two + source[1:-1, 1:-1]
    )


def shade_cells(tracer, open_cells):
    shading = tracer / (1.0 + tracer)
    walls = 1.0 - open_cells
    red = open_cells * shading + 0.55 * walls
    green = open_cells * jnp.exp(-0.5 * tracer) + 0.5 * walls
    blue = open_cells * (0.2 + 0.6 * shading * shading) + 0.45 * walls
    return (red, green, blue)


def composite(nearer, farther):
    colors = nearer[:3] + nearer[3:] * farther[:3]
    return jnp.concatenate([colors, nearer[3:] * farther[3:]], axis=0)


def fold_in_order(layers):
    start_value = jnp.concatenate(
        [
            jnp.zeros((3,) + layers.shape[2:], jnp.float32),
            jnp.ones((1,) + layers.shape[2:], jnp.float32),
        ],
        axis=0,
    )

    def fold_step(running, layer_piece):
        return (composite(running, layer_piece), None)

    result, unused = lax.scan(fold_step, start_value, layers)
    return result


def finish_pixels(result):
    return jnp.concatenate([result[:3], 1.0 - result[3:]], axis=0)


def march_steps(tracer, speeds, open_wide, source_wide):
    current = tracer
    for substep in range(STEPS):
        tracer_wide = padded_2(current, (("view", 0), ("wide", 1)), 1)
        current = advance(tracer_wide, speeds, open_wide, source_wide)
    return current


def on_device(tracer, velocity, buildings, source):
    open_cells = (1 - buildings).astype(jnp.float32)
    static = jnp.concatenate([velocity, open_cells[None], source[None]], axis=0)
    grown_static = padded_2(static, (("view", 1), ("wide", 2)), 1)
    current = march_steps(tracer, grown_static[:3], grown_static[3], grown_static[4])
    view_count = lax.axis_size("view")
    depth_cells = float(tracer.shape[0] * view_count)
    extinction = (current * open_cells + 4.0 * (1.0 - open_cells)) / depth_cells
    before = jnp.cumsum(extinction, axis=0) - extinction
    weight = jnp.exp(-before) * (1.0 - jnp.exp(-extinction))
    red, green, blue = shade_cells(current, open_cells)
    partial_value = jnp.stack(
        [
            jnp.sum(weight * red, axis=0),
            jnp.sum(weight * green, axis=0),
            jnp.sum(weight * blue, axis=0),
            jnp.exp(-jnp.sum(extinction, axis=0)),
        ]
    )
    height = partial_value.shape[2]
    block_width = height // view_count
    position = lax.axis_index("view")
    pieces = lax.all_gather(partial_value[None], "view", axis=0, tiled=True)
    mine = lax.dynamic_slice_in_dim(pieces, position * block_width, block_width, 3)
    picture = finish_pixels(fold_in_order(mine))
    return (current, picture)


def solution(mesh):
    return jax.shard_map(
        on_device,
        mesh=mesh,
        in_specs=(
            P("view", "wide", None),
            P(None, "view", "wide", None),
            P("view", "wide", None),
            P("view", "wide", None),
        ),
        out_specs=(P("view", "wide", None), P(None, "wide", "view")),
        check_vma=False,
    )
```

profile of v0, /device:TPU:32, one launch (start us, length us, event | category | flops | bytes accessed | tf_op | source)
XLA Modules:
  0.0 111.1 jit_solution(14347198532158714569)
XLA Ops:
  1.5 1.8 %collective-permute-start.5 = (f32[1,32,128]{2,1,0:T(8,128)S(1)}, f32[1,32,128]{2,1,0:T(8,128)S(1)}, u32[]{:S(2)}, u32[]{:S(2)}) collective-permute-start(f32[1,32,128]{2,1,0:T(8,128)S(1)} %get-tuple-element.84), channel_id=1, source_target_pairs={{32,0},{64,32},{96,64},{128,96},{160,128},{192,160},{224,192},{0,2... | collective-permute-start | bytes 49160 | tf_op jit(solution)/shard_map/ppermute | solution.py:18
  3.5 1.3 %convert_bitcast_fusion = f32[1,64,32,128]{3,2,1,0:T(8,128)S(1)} fusion(s32[64,32,128]{2,1,0:T(8,128)} %param.8), kind=kLoop, calls=%fused_computation.110 | loop fusion | flops 524288 | bytes 2097152 | tf_op jit(solution)/shard_map/broadcast_in_dim | solution.py:91
  4.9 1.0 pad_maximum_fusion.13
  5.9 2.0 %collective-permute-start = (f32[5,1,32,128]{3,2,1,0:T(8,128)S(1)}, f32[5,1,32,128]{3,2,1,0:T(8,128)S(1)}, u32[]{:S(2)}, u32[]{:S(2)}) collective-permute-start(f32[5,1,32,128]{3,2,1,0:T(8,128)S(1)} %get-tuple-element.44), channel_id=1, source_target_pairs={{0,32},{32,64},{64,96},{96,128},{128,160},{160,192},{192,224},{224... | collective-permute-start | bytes 245768 | tf_op jit(solution)/shard_map/ppermute | solution.py:16
  7.9 2.1 %collective-permute-start.1 = (f32[5,1,32,128]{3,2,1,0:T(8,128)S(1)}, f32[5,1,32,128]{3,2,1,0:T(8,128)S(1)}, u32[]{:S(2)}, u32[]{:S(2)}) collective-permute-start(f32[5,1,32,128]{3,2,1,0:T(8,128)S(1)} %get-tuple-element.45), channel_id=1, source_target_pairs={{32,0},{64,32},{96,64},{128,96},{160,128},{192,160},{224,192},{0,2... | collective-permute-start | bytes 245768 | tf_op jit(solution)/shard_map/ppermute | solution.py:18
  10.2 5.1 %collective-permute-start.7 = (f32[66,1,128]{2,1,0:T(1,128)S(1)}, f32[66,1,128]{2,1,0:T(1,128)S(1)}, u32[]{:S(2)}, u32[]{:S(2)}) collective-permute-start(f32[66,1,128]{2,1,0:T(1,128)S(1)} %get-tuple-element.77), channel_id=1, source_target_pairs={{1,0},{2,1},{3,2},{4,3},{5,4},{6,5},{7,6},{8,7},{9,8},{10,9},{11,1... | collective-permute-start | bytes 101384 | tf_op jit(solution)/shard_map/ppermute | solution.py:18
  15.6 5.1 %collective-permute-start.3 = (f32[5,66,1,128]{3,2,1,0:T(1,128)S(1)}, f32[5,66,1,128]{3,2,1,0:T(1,128)S(1)}, u32[]{:S(2)}, u32[]{:S(2)}) collective-permute-start(f32[5,66,1,128]{3,2,1,0:T(1,128)S(1)} %get-tuple-element.43), channel_id=1, source_target_pairs={{1,0},{2,1},{3,2},{4,3},{5,4},{6,5},{7,6},{8,7},{9,8},{10,9},{11,1... | collective-permute-start | bytes 506888 | tf_op jit(solution)/shard_map/ppermute | solution.py:18
  20.9 2.8 %collective-permute-done.2 = f32[5,66,1,128]{3,2,1,0:T(1,128)S(1)} collective-permute-done((f32[5,66,1,128]{3,2,1,0:T(1,128)S(1)}, f32[5,66,1,128]{3,2,1,0:T(1,128)S(1)}, u32[]{:S(2)}, u32[]{:S(2)}) %collective-permute-start.2) | collective-permute-done | bytes 168992 | tf_op jit(solution)/shard_map/ppermute | solution.py:16
  23.7 2.7 %pad_maximum_fusion.1 = f32[5,66,34,128]{3,2,1,0:T(8,128)S(1)} fusion(f32[5,66,1,128]{3,2,1,0:T(1,128)S(1)} %collective-permute-done.3, f32[5,1,32,128]{3,2,1,0:T(8,128)S(1)} %collective-permute-done.1, f32[1,64,32,128]{3,2,1,0:T(8,128)S(1)} %bitcast.45, f32[1,64,32,128]{3,2,1,0:T(8,128)S(1)} %convert_bitcast_fusion, f32[3,64,32,128]{3,2,1,0:T(8,128)S(1)} %copy-done, ...), kind=kLoop, calls=%fused_computation.7 | loop fusion | flops 8616960 | bytes 11489280 | tf_op jit(solution)/shard_map/concatenate | solution.py:14
  29.5 0.9 fusion.37
  30.4 1.3 %collective-permute-start.8 = (f32[1,32,128]{2,1,0:T(8,128)S(1)}, f32[1,32,128]{2,1,0:T(8,128)S(1)}, u32[]{:S(2)}, u32[]{:S(2)}) collective-permute-start(f32[1,32,128]{2,1,0:T(8,128)S(1)} %get-tuple-element.82), channel_id=1, source_target_pairs={{0,32},{32,64},{64,96},{96,128},{128,160},{160,192},{192,224},{224... | collective-permute-start | bytes 49160 | tf_op jit(solution)/shard_map/ppermute | solution.py:16
  31.7 2.3 %collective-permute-start.9 = (f32[1,32,128]{2,1,0:T(8,128)S(1)}, f32[1,32,128]{2,1,0:T(8,128)S(1)}, u32[]{:S(2)}, u32[]{:S(2)}) collective-permute-start(f32[1,32,128]{2,1,0:T(8,128)S(1)} %get-tuple-element.83), channel_id=1, source_target_pairs={{32,0},{64,32},{96,64},{128,96},{160,128},{192,160},{224,192},{0,2... | collective-permute-start | bytes 49160 | tf_op jit(solution)/shard_map/ppermute | solution.py:18
  34.0 1.6 %collective-permute-done.8 = f32[1,32,128]{2,1,0:T(8,128)S(1)} collective-permute-done((f32[1,32,128]{2,1,0:T(8,128)S(1)}, f32[1,32,128]{2,1,0:T(8,128)S(1)}, u32[]{:S(2)}, u32[]{:S(2)}) %collective-permute-start.8) | collective-permute-done | bytes 16416 | tf_op jit(solution)/shard_map/ppermute | solution.py:16
  35.7 5.1 %collective-permute-start.11 = (f32[66,1,128]{2,1,0:T(1,128)S(1)}, f32[66,1,128]{2,1,0:T(1,128)S(1)}, u32[]{:S(2)}, u32[]{:S(2)}) collective-permute-start(f32[66,1,128]{2,1,0:T(1,128)S(1)} %get-tuple-element.75), channel_id=1, source_target_pairs={{1,0},{2,1},{3,2},{4,3},{5,4},{6,5},{7,6},{8,7},{9,8},{10,9},{11,1... | collective-permute-start | bytes 101384 | tf_op jit(solution)/shard_map/ppermute | solution.py:18
  40.8 1.6 %collective-permute-done.10 = f32[66,1,128]{2,1,0:T(1,128)S(1)} collective-permute-done((f32[66,1,128]{2,1,0:T(1,128)S(1)}, f32[66,1,128]{2,1,0:T(1,128)S(1)}, u32[]{:S(2)}, u32[]{:S(2)}) %collective-permute-start.10) | collective-permute-done | bytes 33824 | tf_op jit(solution)/shard_map/ppermute | solution.py:16
  44.6 1.1 %fusion.32 = f32[64,32,128]{2,1,0:T(8,128)S(1)} fusion(f32[66,34,128]{2,1,0:T(8,128)S(1)} %get-tuple-element.57, f32[66,34,128]{2,1,0:T(8,128)S(1)} %get-tuple-element.56, f32[66,32,128]{2,1,0:T(8,128)S(1)} %get-tuple-element.55, f32[66,32,128]{2,1,0:T(8,128)S(1)} %get-tuple-element.54, f32[64,32,128]{2,1,0:T(8,128)S(1)} %fusion.37, ...), kind=kLoop, calls=%fused_computation.92 | loop fusion | flops 2097152 | bytes 10485760 | tf_op jit(solution)/shard_map/mul | solution.py:42
  45.7 3.0 %collective-permute-start.12 = (f32[1,32,128]{2,1,0:T(8,128)S(1)}, f32[1,32,128]{2,1,0:T(8,128)S(1)}, u32[]{:S(2)}, u32[]{:S(2)}) collective-permute-start(f32[1,32,128]{2,1,0:T(8,128)S(1)} %get-tuple-element.80), channel_id=1, source_target_pairs={{0,32},{32,64},{64,96},{96,128},{128,160},{160,192},{192,224},{224... | collective-permute-start | bytes 49160 | tf_op jit(solution)/shard_map/ppermute | solution.py:16
  49.1 1.6 %collective-permute-done.12 = f32[1,32,128]{2,1,0:T(8,128)S(1)} collective-permute-done((f32[1,32,128]{2,1,0:T(8,128)S(1)}, f32[1,32,128]{2,1,0:T(8,128)S(1)}, u32[]{:S(2)}, u32[]{:S(2)}) %collective-permute-start.12) | collective-permute-done | bytes 16416 | tf_op jit(solution)/shard_map/ppermute | solution.py:16
  50.7 2.9 %collective-permute-done.13 = f32[1,32,128]{2,1,0:T(8,128)S(1)} collective-permute-done((f32[1,32,128]{2,1,0:T(8,128)S(1)}, f32[1,32,128]{2,1,0:T(8,128)S(1)}, u32[]{:S(2)}, u32[]{:S(2)}) %collective-permute-start.13) | collective-permute-done | bytes 16416 | tf_op jit(solution)/shard_map/ppermute | solution.py:18
  53.8 5.1 %collective-permute-start.15 = (f32[66,1,128]{2,1,0:T(1,128)S(1)}, f32[66,1,128]{2,1,0:T(1,128)S(1)}, u32[]{:S(2)}, u32[]{:S(2)}) collective-permute-start(f32[66,1,128]{2,1,0:T(1,128)S(1)} %get-tuple-element.73), channel_id=1, source_target_pairs={{1,0},{2,1},{3,2},{4,3},{5,4},{6,5},{7,6},{8,7},{9,8},{10,9},{11,1... | collective-permute-start | bytes 101384 | tf_op jit(solution)/shard_map/ppermute | solution.py:18
  58.8 1.6 %collective-permute-done.14 = f32[66,1,128]{2,1,0:T(1,128)S(1)} collective-permute-done((f32[66,1,128]{2,1,0:T(1,128)S(1)}, f32[66,1,128]{2,1,0:T(1,128)S(1)}, u32[]{:S(2)}, u32[]{:S(2)}) %collective-permute-start.14) | collective-permute-done | bytes 33824 | tf_op jit(solution)/shard_map/ppermute | solution.py:16
  62.7 1.2 %fusion.27 = f32[64,32,128]{2,1,0:T(8,128)S(1)} fusion(f32[66,34,128]{2,1,0:T(8,128)S(1)} %get-tuple-element.53, f32[66,34,128]{2,1,0:T(8,128)S(1)} %get-tuple-element.52, f32[66,32,128]{2,1,0:T(8,128)S(1)} %get-tuple-element.51, f32[66,32,128]{2,1,0:T(8,128)S(1)} %get-tuple-element.50, f32[64,32,128]{2,1,0:T(8,128)S(1)} %fusion.32, ...), kind=kLoop, calls=%fused_computation.84 | loop fusion | flops 2097152 | bytes 10485760 | tf_op jit(solution)/shard_map/mul | solution.py:42
  63.9 2.1 %collective-permute-start.16 = (f32[1,32,128]{2,1,0:T(8,128)S(1)}, f32[1,32,128]{2,1,0:T(8,128)S(1)}, u32[]{:S(2)}, u32[]{:S(2)}) collective-permute-start(f32[1,32,128]{2,1,0:T(8,128)S(1)} %get-tuple-element.78), channel_id=1, source_target_pairs={{0,32},{32,64},{64,96},{96,128},{128,160},{160,192},{192,224},{224... | collective-permute-start | bytes 49160 | tf_op jit(solution)/shard_map/ppermute | solution.py:16
  66.0 1.7 %collective-permute-done.16 = f32[1,32,128]{2,1,0:T(8,128)S(1)} collective-permute-done((f32[1,32,128]{2,1,0:T(8,128)S(1)}, f32[1,32,128]{2,1,0:T(8,128)S(1)}, u32[]{:S(2)}, u32[]{:S(2)}) %collective-permute-start.16) | collective-permute-done | bytes 16416 | tf_op jit(solution)/shard_map/ppermute | solution.py:16
  67.7 2.0 %collective-permute-done.17 = f32[1,32,128]{2,1,0:T(8,128)S(1)} collective-permute-done((f32[1,32,128]{2,1,0:T(8,128)S(1)}, f32[1,32,128]{2,1,0:T(8,128)S(1)}, u32[]{:S(2)}, u32[]{:S(2)}) %collective-permute-start.17) | collective-permute-done | bytes 16416 | tf_op jit(solution)/shard_map/ppermute | solution.py:18
  69.8 5.1 %collective-permute-start.19 = (f32[66,1,128]{2,1,0:T(1,128)S(1)}, f32[66,1,128]{2,1,0:T(1,128)S(1)}, u32[]{:S(2)}, u32[]{:S(2)}) collective-permute-start(f32[66,1,128]{2,1,0:T(1,128)S(1)} %get-tuple-element.71), channel_id=1, source_target_pairs={{1,0},{2,1},{3,2},{4,3},{5,4},{6,5},{7,6},{8,7},{9,8},{10,9},{11,1... | collective-permute-start | bytes 101384 | tf_op jit(solution)/shard_map/ppermute | solution.py:18
  74.9 1.6 %collective-permute-done.18 = f32[66,1,128]{2,1,0:T(1,128)S(1)} collective-permute-done((f32[66,1,128]{2,1,0:T(1,128)S(1)}, f32[66,1,128]{2,1,0:T(1,128)S(1)}, u32[]{:S(2)}, u32[]{:S(2)}) %collective-permute-start.18) | collective-permute-done | bytes 33824 | tf_op jit(solution)/shard_map/ppermute | solution.py:16
  77.0 1.0 copy-done.6
  78.5 0.9 copy-done.4
  81.5 1.0 fusion.22
  82.7 1.4 %multiply_reduce_fusion.1 = (f32[32,128]{1,0:T(8,128)S(1)}, f32[32,128]{1,0:T(8,128)S(1)}, f32[32,128]{1,0:T(8,128)S(1)}, f32[32,128]{1,0:T(8,128)S(1)}) fusion(s32[64,32,128]{2,1,0:T(8,128)S(1)} %copy-done.10, f32[64,32,128]{2,1,0:T(8,128)S(1)} %fusion.22), kind=kOutput, calls=%fused_computation.106 | output fusion | flops 27246592 | bytes 2162688 | tf_op jit(solution)/shard_map/jit(cumsum)/reduce_window_sum | solution.py:97
  84.1 25.4 %all-gather = f32[32,32,128]{2,1,0:T(8,128)S(1)} all-gather(f32[4,32,128]{2,1,0:T(8,128)S(1)} %pad_maximum_fusion.14), channel_id=2, replica_groups=mesh['view'=8,'wide'=32] {'view'}, dimensions={0}, use_global_device_ids=true | all-gather | bytes 589824 | tf_op jit(solution)/shard_map/all_gather | solution.py:111
  (118 shorter events, 14.9 us)
Async XLA Ops:
  0.6 4.2 %copy-start.11 = (f32[64,32,128]{2,1,0:T(8,128)S(1)}, f32[64,32,128]{2,1,0:T(8,128)}, u32[]{:S(2)}) copy-start(f32[64,32,128]{2,1,0:T(8,128)} %param.9) | copy-start | bytes 3145732
  1.5 8.6 %collective-permute-start.5 = (f32[1,32,128]{2,1,0:T(8,128)S(1)}, f32[1,32,128]{2,1,0:T(8,128)S(1)}, u32[]{:S(2)}, u32[]{:S(2)}) collective-permute-start(f32[1,32,128]{2,1,0:T(8,128)S(1)} %get-tuple-element.84), channel_id=1, source_target_pairs={{32,0},{64,32},{96,64},{128,96},{160,128},{192,160},{224,192},{0,2... | collective-permute-start | bytes 49160 | tf_op jit(solution)/shard_map/ppermute | solution.py:18
  3.3 6.7 %collective-permute-start.4 = (f32[1,32,128]{2,1,0:T(8,128)S(1)}, f32[1,32,128]{2,1,0:T(8,128)S(1)}, u32[]{:S(2)}, u32[]{:S(2)}) collective-permute-start(f32[1,32,128]{2,1,0:T(8,128)S(1)} %get-tuple-element.85), channel_id=1, source_target_pairs={{0,32},{32,64},{64,96},{96,128},{128,160},{160,192},{192,224},{224... | collective-permute-start | bytes 49160 | tf_op jit(solution)/shard_map/ppermute | solution.py:16
  4.8 5.1 %copy-start.12 = (f32[64,32,128]{2,1,0:T(8,128)S(1)}, f32[64,32,128]{2,1,0:T(8,128)}, u32[]{:S(2)}) copy-start(f32[64,32,128]{2,1,0:T(8,128)} %param.6) | copy-start | bytes 3145732
  4.9 10.4 %copy-start = (f32[3,64,32,128]{3,2,1,0:T(8,128)S(1)}, f32[3,64,32,128]{3,2,1,0:T(8,128)}, u32[]{:S(2)}) copy-start(f32[3,64,32,128]{3,2,1,0:T(8,128)} %param.7) | copy-start | bytes 9437188
  5.9 9.4 %collective-permute-start = (f32[5,1,32,128]{3,2,1,0:T(8,128)S(1)}, f32[5,1,32,128]{3,2,1,0:T(8,128)S(1)}, u32[]{:S(2)}, u32[]{:S(2)}) collective-permute-start(f32[5,1,32,128]{3,2,1,0:T(8,128)S(1)} %get-tuple-element.44), channel_id=1, source_target_pairs={{0,32},{32,64},{64,96},{96,128},{128,160},{160,192},{192,224},{224... | collective-permute-start | bytes 245768 | tf_op jit(solution)/shard_map/ppermute | solution.py:16
  7.9 7.4 %collective-permute-start.1 = (f32[5,1,32,128]{3,2,1,0:T(8,128)S(1)}, f32[5,1,32,128]{3,2,1,0:T(8,128)S(1)}, u32[]{:S(2)}, u32[]{:S(2)}) collective-permute-start(f32[5,1,32,128]{3,2,1,0:T(8,128)S(1)} %get-tuple-element.45), channel_id=1, source_target_pairs={{32,0},{64,32},{96,64},{128,96},{160,128},{192,160},{224,192},{0,2... | collective-permute-start | bytes 245768 | tf_op jit(solution)/shard_map/ppermute | solution.py:18
  10.1 10.5 %collective-permute-start.6 = (f32[66,1,128]{2,1,0:T(1,128)S(1)}, f32[66,1,128]{2,1,0:T(1,128)S(1)}, u32[]{:S(2)}, u32[]{:S(2)}) collective-permute-start(f32[66,1,128]{2,1,0:T(1,128)S(1)} %get-tuple-element.76), channel_id=1, source_target_pairs={{0,1},{1,2},{2,3},{3,4},{4,5},{5,6},{6,7},{7,8},{8,9},{9,10},{10,1... | collective-permute-start | bytes 101384 | tf_op jit(solution)/shard_map/ppermute | solution.py:16
  10.2 10.5 %collective-permute-start.7 = (f32[66,1,128]{2,1,0:T(1,128)S(1)}, f32[66,1,128]{2,1,0:T(1,128)S(1)}, u32[]{:S(2)}, u32[]{:S(2)}) collective-permute-start(f32[66,1,128]{2,1,0:T(1,128)S(1)} %get-tuple-element.77), channel_id=1, source_target_pairs={{1,0},{2,1},{3,2},{4,3},{5,4},{6,5},{7,6},{8,7},{9,8},{10,9},{11,1... | collective-permute-start | bytes 101384 | tf_op jit(solution)/shard_map/ppermute | solution.py:18
  15.5 8.2 %collective-permute-start.2 = (f32[5,66,1,128]{3,2,1,0:T(1,128)S(1)}, f32[5,66,1,128]{3,2,1,0:T(1,128)S(1)}, u32[]{:S(2)}, u32[]{:S(2)}) collective-permute-start(f32[5,66,1,128]{3,2,1,0:T(1,128)S(1)} %get-tuple-element.42), channel_id=1, source_target_pairs={{0,1},{1,2},{2,3},{3,4},{4,5},{5,6},{6,7},{7,8},{8,9},{9,10},{10,1... | collective-permute-start | bytes 506888 | tf_op jit(solution)/shard_map/ppermute | solution.py:16
  15.6 8.1 %collective-permute-start.3 = (f32[5,66,1,128]{3,2,1,0:T(1,128)S(1)}, f32[5,66,1,128]{3,2,1,0:T(1,128)S(1)}, u32[]{:S(2)}, u32[]{:S(2)}) collective-permute-start(f32[5,66,1,128]{3,2,1,0:T(1,128)S(1)} %get-tuple-element.43), channel_id=1, source_target_pairs={{1,0},{2,1},{3,2},{4,3},{5,4},{6,5},{7,6},{8,7},{9,8},{10,9},{11,1... | collective-permute-start | bytes 506888 | tf_op jit(solution)/shard_map/ppermute | solution.py:18
  26.9 35.8 %copy-start.1 = (f32[66,34,128]{2,1,0:T(8,128)}, f32[66,34,128]{2,1,0:T(8,128)S(1)}, u32[]{:S(2)}) copy-start(f32[66,34,128]{2,1,0:T(8,128)S(1)} %get-tuple-element.38) | copy-start | bytes 3446788
  27.2 33.5 %copy-start.7 = (f32[1,65,34,128]{3,2,1,0:T(8,128)}, f32[1,65,34,128]{3,2,1,0:T(8,128)S(1)}, u32[]{:S(2)}) copy-start(f32[1,65,34,128]{3,2,1,0:T(8,128)S(1)} %get-tuple-element.31) | copy-start | bytes 3394564
  27.7 33.7 %copy-start.3 = (f32[66,33,128]{2,1,0:T(8,128)}, f32[66,33,128]{2,1,0:T(8,128)S(1)}, u32[]{:S(2)}) copy-start(f32[66,33,128]{2,1,0:T(8,128)S(1)} %get-tuple-element.33) | copy-start | bytes 3345412
  29.0 31.9 %copy-start.5 = (f32[66,34,127]{2,1,0:T(8,128)}, f32[66,34,127]{2,1,0:T(8,128)S(1)}, u32[]{:S(2)}) copy-start(f32[66,34,127]{2,1,0:T(8,128)S(1)} %get-tuple-element.35) | copy-start | bytes 3419860
  30.4 5.2 %collective-permute-start.8 = (f32[1,32,128]{2,1,0:T(8,128)S(1)}, f32[1,32,128]{2,1,0:T(8,128)S(1)}, u32[]{:S(2)}, u32[]{:S(2)}) collective-permute-start(f32[1,32,128]{2,1,0:T(8,128)S(1)} %get-tuple-element.82), channel_id=1, source_target_pairs={{0,32},{32,64},{64,96},{96,128},{128,160},{160,192},{192,224},{224... | collective-permute-start | bytes 49160 | tf_op jit(solution)/shard_map/ppermute | solution.py:16
  31.7 3.9 %collective-permute-start.9 = (f32[1,32,128]{2,1,0:T(8,128)S(1)}, f32[1,32,128]{2,1,0:T(8,128)S(1)}, u32[]{:S(2)}, u32[]{:S(2)}) collective-permute-start(f32[1,32,128]{2,1,0:T(8,128)S(1)} %get-tuple-element.83), channel_id=1, source_target_pairs={{32,0},{64,32},{96,64},{128,96},{160,128},{192,160},{224,192},{0,2... | collective-permute-start | bytes 49160 | tf_op jit(solution)/shard_map/ppermute | solution.py:18
  35.7 6.7 %collective-permute-start.10 = (f32[66,1,128]{2,1,0:T(1,128)S(1)}, f32[66,1,128]{2,1,0:T(1,128)S(1)}, u32[]{:S(2)}, u32[]{:S(2)}) collective-permute-start(f32[66,1,128]{2,1,0:T(1,128)S(1)} %get-tuple-element.74), channel_id=1, source_target_pairs={{0,1},{1,2},{2,3},{3,4},{4,5},{5,6},{6,7},{7,8},{8,9},{9,10},{10,1... | collective-permute-start | bytes 101384 | tf_op jit(solution)/shard_map/ppermute | solution.py:16
  35.7 6.7 %collective-permute-start.11 = (f32[66,1,128]{2,1,0:T(1,128)S(1)}, f32[66,1,128]{2,1,0:T(1,128)S(1)}, u32[]{:S(2)}, u32[]{:S(2)}) collective-permute-start(f32[66,1,128]{2,1,0:T(1,128)S(1)} %get-tuple-element.75), channel_id=1, source_target_pairs={{1,0},{2,1},{3,2},{4,3},{5,4},{6,5},{7,6},{8,7},{9,8},{10,9},{11,1... | collective-permute-start | bytes 101384 | tf_op jit(solution)/shard_map/ppermute | solution.py:18
  45.7 5.0 %collective-permute-start.12 = (f32[1,32,128]{2,1,0:T(8,128)S(1)}, f32[1,32,128]{2,1,0:T(8,128)S(1)}, u32[]{:S(2)}, u32[]{:S(2)}) collective-permute-start(f32[1,32,128]{2,1,0:T(8,128)S(1)} %get-tuple-element.80), channel_id=1, source_target_pairs={{0,32},{32,64},{64,96},{96,128},{128,160},{160,192},{192,224},{224... | collective-permute-start | bytes 49160 | tf_op jit(solution)/shard_map/ppermute | solution.py:16
  48.7 4.9 %collective-permute-start.13 = (f32[1,32,128]{2,1,0:T(8,128)S(1)}, f32[1,32,128]{2,1,0:T(8,128)S(1)}, u32[]{:S(2)}, u32[]{:S(2)}) collective-permute-start(f32[1,32,128]{2,1,0:T(8,128)S(1)} %get-tuple-element.81), channel_id=1, source_target_pairs={{32,0},{64,32},{96,64},{128,96},{160,128},{192,160},{224,192},{0,2... | collective-permute-start | bytes 49160 | tf_op jit(solution)/shard_map/ppermute | solution.py:18
  53.7 6.7 %collective-permute-start.14 = (f32[66,1,128]{2,1,0:T(1,128)S(1)}, f32[66,1,128]{2,1,0:T(1,128)S(1)}, u32[]{:S(2)}, u32[]{:S(2)}) collective-permute-start(f32[66,1,128]{2,1,0:T(1,128)S(1)} %get-tuple-element.72), channel_id=1, source_target_pairs={{0,1},{1,2},{2,3},{3,4},{4,5},{5,6},{6,7},{7,8},{8,9},{9,10},{10,1... | collective-permute-start | bytes 101384 | tf_op jit(solution)/shard_map/ppermute | solution.py:16
  53.8 6.7 %collective-permute-start.15 = (f32[66,1,128]{2,1,0:T(1,128)S(1)}, f32[66,1,128]{2,1,0:T(1,128)S(1)}, u32[]{:S(2)}, u32[]{:S(2)}) collective-permute-start(f32[66,1,128]{2,1,0:T(1,128)S(1)} %get-tuple-element.73), channel_id=1, source_target_pairs={{1,0},{2,1},{3,2},{4,3},{5,4},{6,5},{7,6},{8,7},{9,8},{10,9},{11,1... | collective-permute-start | bytes 101384 | tf_op jit(solution)/shard_map/ppermute | solution.py:18
  63.9 3.8 %collective-permute-start.16 = (f32[1,32,128]{2,1,0:T(8,128)S(1)}, f32[1,32,128]{2,1,0:T(8,128)S(1)}, u32[]{:S(2)}, u32[]{:S(2)}) collective-permute-start(f32[1,32,128]{2,1,0:T(8,128)S(1)} %get-tuple-element.78), channel_id=1, source_target_pairs={{0,32},{32,64},{64,96},{96,128},{128,160},{160,192},{192,224},{224... | collective-permute-start | bytes 49160 | tf_op jit(solution)/shard_map/ppermute | solution.py:16
  66.0 3.7 %collective-permute-start.17 = (f32[1,32,128]{2,1,0:T(8,128)S(1)}, f32[1,32,128]{2,1,0:T(8,128)S(1)}, u32[]{:S(2)}, u32[]{:S(2)}) collective-permute-start(f32[1,32,128]{2,1,0:T(8,128)S(1)} %get-tuple-element.79), channel_id=1, source_target_pairs={{32,0},{64,32},{96,64},{128,96},{160,128},{192,160},{224,192},{0,2... | collective-permute-start | bytes 49160 | tf_op jit(solution)/shard_map/ppermute | solution.py:18
  69.7 6.7 %collective-permute-start.18 = (f32[66,1,128]{2,1,0:T(1,128)S(1)}, f32[66,1,128]{2,1,0:T(1,128)S(1)}, u32[]{:S(2)}, u32[]{:S(2)}) collective-permute-start(f32[66,1,128]{2,1,0:T(1,128)S(1)} %get-tuple-element.70), channel_id=1, source_target_pairs={{0,1},{1,2},{2,3},{3,4},{4,5},{5,6},{6,7},{7,8},{8,9},{9,10},{10,1... | collective-permute-start | bytes 101384 | tf_op jit(solution)/shard_map/ppermute | solution.py:16
  69.8 6.7 %collective-permute-start.19 = (f32[66,1,128]{2,1,0:T(1,128)S(1)}, f32[66,1,128]{2,1,0:T(1,128)S(1)}, u32[]{:S(2)}, u32[]{:S(2)}) collective-permute-start(f32[66,1,128]{2,1,0:T(1,128)S(1)} %get-tuple-element.71), channel_id=1, source_target_pairs={{1,0},{2,1},{3,2},{4,3},{5,4},{6,5},{7,6},{8,7},{9,8},{10,9},{11,1... | collective-permute-start | bytes 101384 | tf_op jit(solution)/shard_map/ppermute | solution.py:18
  74.9 1.8 %copy-start.8 = (f32[1,65,34,128]{3,2,1,0:T(8,128)S(1)}, f32[1,65,34,128]{3,2,1,0:T(8,128)}, u32[]{:S(2)}) copy-start(f32[1,65,34,128]{3,2,1,0:T(8,128)} %copy-done.7) | copy-start | bytes 3394564
  76.7 1.3 %copy-start.6 = (f32[66,34,127]{2,1,0:T(8,128)S(1)}, f32[66,34,127]{2,1,0:T(8,128)}, u32[]{:S(2)}) copy-start(f32[66,34,127]{2,1,0:T(8,128)} %copy-done.5) | copy-start | bytes 3419860
  80.2 1.3 %copy-start.2 = (f32[66,34,128]{2,1,0:T(8,128)S(1)}, f32[66,34,128]{2,1,0:T(8,128)}, u32[]{:S(2)}) copy-start(f32[66,34,128]{2,1,0:T(8,128)} %copy-done.1) | copy-start | bytes 3446788
  82.7 1.4 %copy-start.9 = (f32[64,32,128]{2,1,0:T(8,128)}, f32[64,32,128]{2,1,0:T(8,128)S(1)}, u32[]{:S(2)}) copy-start(f32[64,32,128]{2,1,0:T(8,128)S(1)} %fusion.22) | copy-start | bytes 3145732
  84.1 25.8 %copy-start.13 = (f32[4,32,16]{1,2,0:T(8,128)S(1)}, f32[4,32,16]{1,2,0:T(8,128)}, u32[]{:S(2)}) copy-start(f32[4,32,16]{1,2,0:T(8,128)} %constant.9.clone.1) | copy-start | bytes 24580
  (2 other events, 2.6 us)
where the time goes:
time: 111 us
  starting transfers between devices  40.9 us (37%)
  blocking collectives  25.4 us (23%)
  other arithmetic  17.7 us (16%)
  waiting for transfers between devices  17.6 us (16%)
  local copies, waits for them, and re-layouts  8.11 us (7%)
  between operations  1.16 us (1%)
    ppermute x10, starting transfers between devices, padded_2(): lax.ppermute(head, axis, [((i + 1) % count, i) for i in range(count)])  31.9 us
    all_gather x1, blocking collectives, on_device(): pieces = lax.all_gather(partial_value[None], 'view', axis=0, tiled=True)  25.4 us
    ppermute x10, waiting for transfers between devices, padded_2(): lax.ppermute(tail, axis, [(i, (i + 1) % count) for i in range(count)])  12.6 us
    ppermute x10, starting transfers between devices, padded_2(): lax.ppermute(tail, axis, [(i, (i + 1) % count) for i in range(count)])  8.96 us
    ppermute x10, waiting for transfers between devices, padded_2(): lax.ppermute(head, axis, [((i + 1) % count, i) for i in range(count)])  4.99 us
    mul x4, other arithmetic, advance(): open_cells[1:-1, 1:-1]  4.2 us
    concatenate x5, other arithmetic, padded_2(): jnp.concatenate([lax.ppermute(tail, axis, [(i, (i + 1) % count) for i in...  3.6 us
    unnamed x31, local copies, waits for them, and re-layouts  3.31 us
  transfers between devices with their start and end apart: 20, of which 9 were waited for; matrix products, arithmetic and copies ran while one was open for 3% of the time, Pallas kernels for 0%

commit v1 on v0

v1 whole, which is shorter than its diff:
```python
import functools
import math

import jax
import jax.numpy as jnp
from jax import lax
from jax.experimental import pallas as pl
from jax.experimental.pallas import tpu as pltpu
from jax.sharding import PartitionSpec as P

STEPS = 4
H = STEPS
Y0 = 8
MESH = pl.DeviceIdType.MESH
LOG2E = math.log2(math.e)
UNROLL = 8


def sweep(start, count, body, carry, unroll=UNROLL):
    trips = count // unroll

    def chunk(trip, carry):
        first = start + trip * unroll
        for offset in range(unroll):
            carry = body(first + offset, carry)
        return carry

    if trips > 1:
        carry = lax.fori_loop(0, trips, chunk, carry)
    elif trips == 1:
        carry = chunk(0, carry)
    for offset in range(trips * unroll, count):
        carry = body(start + offset, carry)
    return carry


def flux(speed, lower, upper):
    return jnp.where(speed > 0.0, lower, upper) * speed


def face_range(side, size, depth):
    if side == 0:
        return 0, 0, size
    if side > 0:
        return size - depth, -depth, depth
    return 0, size, depth


def kernel(
    nx, ny, nz, views, wides,
    tracer, velocity, buildings, source,
    out, picture,
    t_raw, v_raw, b_raw, s_raw, wx, wy, wz, src, c0, c1, c2, c3, c4,
    acc, mid_acc, part, pieces,
    local_sem, out_sem, send_sem, recv_sem, piece_send, piece_recv,
):
    my_view, my_wide = lax.axis_index("view"), lax.axis_index("wide")

    def device(dv, dw):
        return (lax.rem(my_view + dv + views, views), lax.rem(my_wide + dw + wides, wides))

    neighbours = [(dv, dw) for dv in (0, 1, -1) for dw in (0, 1, -1) if (dv, dw) != (0, 0)]
    far = [(dv, 0) for dv in range(2, views - 1)]

    own_planes, own_rows = pl.ds(H + 1, nx), pl.ds(Y0, ny)
    loads = [
        pltpu.make_async_copy(buildings, b_raw.at[own_planes, own_rows], local_sem.at[0]),
        pltpu.make_async_copy(velocity, v_raw.at[:, own_planes, own_rows], local_sem.at[1]),
        pltpu.make_async_copy(tracer, t_raw.at[own_planes, own_rows], local_sem.at[2]),
        pltpu.make_async_copy(source, s_raw.at[own_planes, own_rows], local_sem.at[3]),
    ]
    for load in loads:
        load.start()

    barrier = pltpu.get_barrier_semaphore()
    for dv, dw in neighbours + far:
        pl.semaphore_signal(barrier, inc=1, device_id=device(dv, dw), device_id_type=MESH)
    pl.semaphore_wait(barrier, len(neighbours) + len(far))

    sends = []

    def send(ref, buffer, dv, dw, depth, pick=None):
        xs, xd, xn = face_range(dv, nx, depth)
        ys, yd, yn = face_range(dw, ny, depth)
        here = (pl.ds(xs, xn), pl.ds(ys, yn))
        there = (pl.ds(xd + H + 1, xn), pl.ds(yd + Y0, yn))
        if pick is not None:
            here, there = (pick,) + here, (pick,) + there
        index = len(sends)
        copy = pltpu.make_async_remote_copy(
            src_ref=ref.at[here], dst_ref=buffer.at[there],
            send_sem=send_sem.at[index], recv_sem=recv_sem.at[index],
            device_id=device(dv, dw), device_id_type=MESH,
        )
        copy.start()
        sends.append(copy)

    for dv, dw in sorted(neighbours, key=lambda n: -abs(n[0]) - 2 * abs(n[0] * n[1])):
        corner = dv != 0 and dw != 0
        send(buildings, b_raw, dv, dw, H - 1 if corner else H)
        send(tracer, t_raw, dv, dw, H - 1 if corner else H)
        if (dv, dw) == (1, 0):
            send(velocity, v_raw, dv, dw, H, pl.ds(0, 1))
            send(velocity, v_raw, dv, dw, H - 1, pl.ds(1, 2))
        elif (dv, dw) == (0, 1):
            send(velocity, v_raw, dv, dw, H, pl.ds(1, 1))
            send(velocity, v_raw, dv, dw, H - 1, pl.ds(0, 1))
            send(velocity, v_raw, dv, dw, H - 1, pl.ds(2, 1))
        else:
            send(velocity, v_raw, dv, dw, H - 1, pl.ds(0, 3))
        send(source, s_raw, dv, dw, H - 2 if corner else H - 1)

    levels = (c0, c1, c2, c3, c4)
    below_top = lax.broadcasted_iota(jnp.int32, (1, nz), 1) < nz - 1

    def prepare(first, count, row, rows, shift):
        here, up = pl.ds(row, rows), pl.ds(row + 1, rows)

        def body(p, b_here):
            b_next = b_raw[p + 1, here, :]
            b_up = pltpu.roll(b_here, rows - 1, 0) if shift == "roll" else b_raw[p, up, :]
            open_here = b_here == 0
            wx[p, here, :] = jnp.where((b_here | b_next) == 0, v_raw[0, p, here, :], 0.0)
            wy[p, here, :] = jnp.where((b_here | b_up) == 0, v_raw[1, p, here, :], 0.0)
            wz[p, here, :] = jnp.where(open_here & below_top, v_raw[2, p, here, :], 0.0)
            src[p, here, :] = jnp.where(open_here, s_raw[p, here, :], 0.0)
            c0[p, here, :] = jnp.where(open_here, t_raw[p, here, :], 0.0)
            return b_next

        sweep(first, count, body, b_raw[first, here, :])

    def advance(step, first, count, row, rows, shift, shade=None, carry=()):
        old, new = levels[step - 1], levels[step]
        here, up, low = pl.ds(row, rows), pl.ds(row + 1, rows), pl.ds(row - 1, rows)

        def body(p, state):
            here_c, flux_low, carry = state
            next_c = old[p + 1, here, :]
            flux_x = flux(wx[p, here, :], here_c, next_c)
            wy_here = wy[p, here, :]
            if shift == "roll":
                flux_y = flux(wy_here, here_c, pltpu.roll(here_c, rows - 1, 0))
                flux_y_low = pltpu.roll(flux_y, 1, 0)
            else:
                flux_y = flux(wy_here, here_c, old[p, up, :])
                flux_y_low = flux(wy[p, low, :], old[p, low, :], here_c)
            flux_z = flux(wz[p, here, :], here_c, pltpu.roll(here_c, nz - 1, 1))
            flux_z_low = pltpu.roll(flux_z, 1, 1)
            value = here_c + src[p, here, :] - (flux_x - flux_low) - (flux_y - flux_y_low) - (flux_z - flux_z_low)
            new[p, here, :] = value
            if shade is not None:
                carry = shade(value, b_raw[p, here, :], carry)
            return next_c, flux_x, carry

        here_c = old[first, here, :]
        flux_low = flux(wx[first - 1, here, :], old[first - 1, here, :], here_c)
        return sweep(first, count, body, (here_c, flux_low, carry))[2]

    scale = LOG2E / (nx * views)

    def shade(value, built, carry):
        depth, through, red, green, blue = carry
        wall = built != 0
        depth = depth + jnp.where(wall, 4.0, value) * scale
        after = jnp.exp2(-depth)
        weight = through - after
        shading = value / (1.0 + value)
        red = red + weight * jnp.where(wall, 0.55, shading)
        green = green + weight * jnp.where(wall, 0.5, jnp.exp2(value * (-0.5 * LOG2E)))
        blue = blue + weight * jnp.where(wall, 0.45, 0.2 + 0.6 * (shading * shading))
        return depth, after, red, green, blue

    def nothing(rows):
        zero = jnp.zeros((rows, nz), jnp.float32)
        return zero, jnp.ones((rows, nz), jnp.float32), zero, zero, zero

    x0 = H + 1
    for load in loads:
        load.wait()
    prepare(x0, nx - 1, Y0, ny, "roll")
    last = x0 + nx - 1
    c0[last, own_rows, :] = jnp.where(b_raw[last, own_rows, :] == 0, t_raw[last, own_rows, :], 0.0)
    for step in range(1, STEPS):
        advance(step, x0 + step, nx - 2 * step, Y0, ny, "roll")
    middle = ny - 2 * H
    carry = advance(STEPS, x0 + STEPS, nx - 2 * STEPS, Y0 + H, middle, "load", shade, nothing(middle))
    for i in range(5):
        mid_acc[i] = carry[i]

    for copy in sends:
        copy.wait_recv()
    y_first, wide_rows = Y0 - H, ny + 2 * H
    prepare(1, H, y_first, wide_rows, "load")
    prepare(x0 + nx - 1, H + 1, y_first, wide_rows, "load")
    edges = ((Y0 - H, 2 * H), (Y0 + ny - H, 2 * H))
    for row, rows in edges:
        prepare(x0, nx - 1, row, rows, "load")
    for step in range(1, STEPS):
        advance(step, x0 - H + step, H, y_first, wide_rows, "load")
        for row, rows in edges:
            advance(step, x0 + step, nx - 2 * step, row, rows, "load")
        advance(step, x0 + nx - step, H, y_first, wide_rows, "load")
    carry = advance(STEPS, x0, H, y_first, wide_rows, "load", shade, nothing(wide_rows))
    for i in range(5):
        acc[i] = carry[i]
    for row, rows in edges:
        carry = tuple(acc[i, row - y_first:row - y_first + rows] for i in range(5))
        carry = advance(STEPS, x0 + H, nx - 2 * H, row, rows, "load", shade, carry)
        for i in range(5):
            acc[i, row - y_first:row - y_first + rows] = carry[i]
    inner = slice(2 * H, 2 * H + middle)
    front = acc[1, inner]
    for i in (2, 3, 4):
        acc[i, inner] = acc[i, inner] + front * mid_acc[i]
    depth = acc[0, inner] + mid_acc[0]
    acc[0, inner] = depth
    acc[1, inner] = jnp.exp2(-depth)
    carry = tuple(acc[i] for i in range(5))
    carry = advance(STEPS, x0 + nx - H, H, y_first, wide_rows, "load", shade, carry)
    for i in range(5):
        acc[i] = carry[i]

    store = pltpu.make_async_copy(c4.at[own_planes, own_rows], out, out_sem)
    store.start()

    stacked = jnp.concatenate([acc[i, H:H + ny] for i in (2, 3, 4, 1)], axis=0)
    part[...] = stacked.T
    share = nz // views
    copies = []
    for hop in range(1, views):
        target = lax.rem(my_view + hop, views)
        copy = pltpu.make_async_remote_copy(
            src_ref=part.at[pl.ds(pl.multiple_of(target * share, share), share)],
            dst_ref=pieces.at[my_view],
            send_sem=piece_send.at[hop - 1], recv_sem=piece_recv.at[hop - 1],
            device_id=device(hop, 0), device_id_type=MESH,
        )
        copy.start()
        copies.append(copy)
    pieces[my_view] = part[pl.ds(pl.multiple_of(my_view * share, share), share), :]
    for copy in copies:
        copy.wait_recv()
    lane = lax.broadcasted_iota(jnp.int32, (share, 4 * ny), 1)
    colors = jnp.zeros((share, 4 * ny), jnp.float32)
    through = jnp.ones((share, 4 * ny), jnp.float32)
    for brick in range(views):
        piece = pieces[brick]
        spread = piece
        for group in range(3):
            turned = pltpu.roll(piece, (group + 1) * ny, 1)
            spread = jnp.where(lane // ny == group, turned, spread)
        colors = colors + through * piece
        through = through * spread
    pixels = jnp.where(lane < 3 * ny, colors, 1.0 - through)
    for i in range(4):
        picture[i] = pixels[:, i * ny:(i + 1) * ny]

    for copy in sends + copies:
        copy.wait_send()
    store.wait()


def on_device(tracer, velocity, buildings, source):
    nx, ny, nz = tracer.shape
    views, wides = lax.axis_size("view"), lax.axis_size("wide")
    field = (nx + 2 * H + 2, ny + 2 * Y0, nz)
    buffer = pltpu.VMEM(field, jnp.float32)
    n_sends = 40
    tracer_next, picture = pl.pallas_call(
        functools.partial(kernel, nx, ny, nz, views, wides),
        out_shape=(
            jax.ShapeDtypeStruct((nx, ny, nz), jnp.float32),
            jax.ShapeDtypeStruct((4, nz // views, ny), jnp.float32),
        ),
        in_specs=[pl.BlockSpec(memory_space=pltpu.HBM)] * 4,
        out_specs=(pl.BlockSpec(memory_space=pltpu.HBM), pl.BlockSpec(memory_space=pltpu.VMEM)),
        scratch_shapes=[
            buffer,
            pltpu.VMEM((3,) + field, jnp.float32),
            pltpu.VMEM(field, jnp.int32),
        ]
        + [buffer] * 10
        + [
            pltpu.VMEM((5, ny + 2 * H, nz), jnp.float32),
            pltpu.VMEM((5, ny - 2 * H, nz), jnp.float32),
            pltpu.VMEM((nz, 4 * ny), jnp.float32),
            pltpu.VMEM((views, nz // views, 4 * ny), jnp.float32),
            pltpu.SemaphoreType.DMA((4,)),
            pltpu.SemaphoreType.DMA,
            pltpu.SemaphoreType.DMA((n_sends,)),
            pltpu.SemaphoreType.DMA((n_sends,)),
            pltpu.SemaphoreType.DMA((views - 1,)),
            pltpu.SemaphoreType.DMA((views - 1,)),
        ],
        compiler_params=pltpu.CompilerParams(
            collective_id=0, has_side_effects=True, vmem_limit_bytes=60 * 1024 * 1024
        ),
    )(tracer, velocity, buildings, source)
    return tracer_next, jnp.swapaxes(picture, 1, 2)


def solution(mesh):
    return jax.shard_map(
        on_device,
        mesh=mesh,
        in_specs=(
            P("view", "wide", None),
            P(None, "view", "wide", None),
            P("view", "wide", None),
            P("view", "wide", None),
        ),
        out_specs=(P("view", "wide", None), P(None, "wide", "view")),
        check_vma=False,
    )
```

time: 111 us -> 40.5 us (0.36)
  starting transfers between devices: 40.9 us -> 0 us
  Pallas kernels: 0 us -> 36 us
  blocking collectives: 25.4 us -> 0 us
  other arithmetic: 17.7 us -> 0 us
  waiting for transfers between devices: 17.6 us -> 0 us
  local copies, waits for them, and re-layouts: 8.11 us -> 3.64 us
    ppermute x20 -> x0, starting transfers between devices: 40.9 us -> none  [the longest x10 31.9 us: padded_2(): lax.ppermute(head, axis, [((i + 1) % count, i) for i in range(count)])]
    pallas_call x0 -> x1, Pallas kernels: none -> 36 us  [on_device(): pl.pallas_call(functools.partial(kernel, nx, ny, nz, views, wides), out_s...]
    all_gather x1 -> x0, blocking collectives: 25.4 us -> none  [on_device(): pieces = lax.all_gather(partial_value[None], 'view', axis=0, tiled=True)]
    ppermute x20 -> x0, waiting for transfers between devices: 17.6 us -> none  [the longest x10 12.6 us: padded_2(): lax.ppermute(tail, axis, [(i, (i + 1) % count) for i in range(count)])]
    add x20 -> x0, other arithmetic: 5.04 us -> none  [the longest x4 2.21 us: advance(): jnp.maximum(face_two, 0.0) * tracer[:, :, :-1]]
    mul x12 -> x0, other arithmetic: 4.29 us -> none  [the longest x4 4.2 us: advance(): open_cells[1:-1, 1:-1]]
    concatenate x14 -> x0, other arithmetic: 4.27 us -> none  [the longest x5 3.6 us: padded_2(): jnp.concatenate([lax.ppermute(tail, axis, [(i, (i + 1) % count) for i in...]
    slice x18 -> x0, local copies, waits for them, and re-layouts: 4.24 us -> none  [the longest x4 1.76 us: advance(): delta_two = (padded[:, :, 1:] - padded[:, :, :-1])[1:-1, 1:-1]]
  transfers between devices with their start and end apart: 20 -> 0, of which waited for: 9 -> 0; matrix products, arithmetic and copies ran while one was open for 3% -> 0% of each run, Pallas kernels for 0% -> 0%
where the time goes in v1:
time: 40.5 us; the launch traced here: 40.3 us
  Pallas kernels  36 us (89%)
  local copies, waits for them, and re-layouts  3.64 us (9%)
  between operations  0.64 us (2%)
    pallas_call x1, Pallas kernels, on_device(): pl.pallas_call(functools.partial(kernel, nx, ny, nz, views, wides), out_s...  36 us
    unnamed x2, local copies, waits for them, and re-layouts  3.64 us

profile of v1, /device:TPU:32, one launch (start us, length us, event | category | flops | bytes accessed | tf_op | source)
XLA Modules:
  0.0 40.3 jit_solution(15475325138304134325)
XLA Ops:
  0.6 36.0 %shard_map.59 = (f32[64,32,128]{2,1,0:T(8,128)}, f32[4,16,32]{2,1,0:T(8,128)}) custom-call(f32[64,32,128]{2,1,0:T(8,128)} %tracer.1, f32[3,64,32,128]{3,2,1,0:T(8,128)} %velocity.1, s32[64,32,128]{2,1,0:T(8,128)} %buildings.1, f32[64,32,128]{2,1,0:T(8,128)} %source.1), custom_call_target="tpu_custom_call" | custom-call | tf_op jit(solution)/shard_map/pallas_call | solution.py:269
  36.7 2.3 %copy.8 = f32[64,32,128]{2,1,0:T(8,128)} copy(f32[64,32,128]{2,1,0:T(8,128)} %get-tuple-element.8) | data formatting | bytes 2097152
  38.9 1.4 %copy.9 = f32[4,32,16]{1,2,0:T(8,128)} copy(f32[4,32,16]{1,2,0:T(8,128)} %bitcast.1) | data formatting | bytes 16384

commit v2 on v1

--- a/solution.py
+++ b/solution.py
@@ -13,10 +13,9 @@
 Y0 = 8
 MESH = pl.DeviceIdType.MESH
 LOG2E = math.log2(math.e)
-UNROLL = 8
-
-
-def sweep(start, count, body, carry, unroll=UNROLL):
+
+
+def sweep(start, count, unroll, body, carry):
     trips = count // unroll
 
     def chunk(trip, carry):
@@ -113,12 +112,14 @@
     levels = (c0, c1, c2, c3, c4)
     below_top = lax.broadcasted_iota(jnp.int32, (1, nz), 1) < nz - 1
 
-    def prepare(first, count, row, rows, shift):
-        here, up = pl.ds(row, rows), pl.ds(row + 1, rows)
-
-        def body(p, b_here):
+    def prepare(first, count, windows, unroll, shift="load"):
+        def body(p, built):
+            return tuple(cells(p, row, rows, b_here) for (row, rows), b_here in zip(windows, built))
+
+        def cells(p, row, rows, b_here):
+            here = pl.ds(row, rows)
             b_next = b_raw[p + 1, here, :]
-            b_up = pltpu.roll(b_here, rows - 1, 0) if shift == "roll" else b_raw[p, up, :]
+            b_up = pltpu.roll(b_here, rows - 1, 0) if shift == "roll" else b_raw[p, pl.ds(row + 1, rows), :]
             open_here = b_here == 0
             wx[p, here, :] = jnp.where((b_here | b_next) == 0, v_raw[0, p, here, :], 0.0)
             wy[p, here, :] = jnp.where((b_here | b_up) == 0, v_raw[1, p, here, :], 0.0)
@@ -127,14 +128,17 @@
             c0[p, here, :] = jnp.where(open_here, t_raw[p, here, :], 0.0)
             return b_next
 
-        sweep(first, count, body, b_raw[first, here, :])
-
-    def advance(step, first, count, row, rows, shift, shade=None, carry=()):
+        sweep(first, count, unroll, body, tuple(b_raw[first, pl.ds(row, rows), :] for row, rows in windows))
+
+    def advance(step, first, count, windows, unroll, shift="load", shade=None, carries=None):
         old, new = levels[step - 1], levels[step]
-        here, up, low = pl.ds(row, rows), pl.ds(row + 1, rows), pl.ds(row - 1, rows)
-
-        def body(p, state):
+
+        def body(p, states):
+            return tuple(cells(p, row, rows, state) for (row, rows), state in zip(windows, states))
+
+        def cells(p, row, rows, state):
             here_c, flux_low, carry = state
+            here, up, low = pl.ds(row, rows), pl.ds(row + 1, rows), pl.ds(row - 1, rows)
             next_c = old[p + 1, here, :]
             flux_x = flux(wx[p, here, :], here_c, next_c)
             wy_here = wy[p, here, :]
@@ -152,9 +156,13 @@
                 carry = shade(value, b_raw[p, here, :], carry)
             return next_c, flux_x, carry
 
-        here_c = old[first, here, :]
-        flux_low = flux(wx[first - 1, here, :], old[first - 1, here, :], here_c)
-        return sweep(first, count, body, (here_c, flux_low, carry))[2]
+        states = []
+        for i, (row, rows) in enumerate(windows):
+            here = pl.ds(row, rows)
+            here_c = old[first, here, :]
+            flux_low = flux(wx[first - 1, here, :], old[first - 1, here, :], here_c)
+            states.append((here_c, flux_low, carries[i] if carries else ()))
+        return tuple(state[2] for state in sweep(first, count, unroll, body, tuple(states)))
 
     scale = LOG2E / (nx * views)
 
@@ -175,50 +183,37 @@
         return zero, jnp.ones((rows, nz), jnp.float32), zero, zero, zero
 
     x0 = H + 1
+    last = x0 + nx - 1
     for load in loads:
         load.wait()
-    prepare(x0, nx - 1, Y0, ny, "roll")
-    last = x0 + nx - 1
+    own, middle = [(Y0, ny)], [(Y0 + H, ny - 2 * H)]
+    prepare(x0, nx - 1, own, 8, "roll")
     c0[last, own_rows, :] = jnp.where(b_raw[last, own_rows, :] == 0, t_raw[last, own_rows, :], 0.0)
     for step in range(1, STEPS):
-        advance(step, x0 + step, nx - 2 * step, Y0, ny, "roll")
-    middle = ny - 2 * H
-    carry = advance(STEPS, x0 + STEPS, nx - 2 * STEPS, Y0 + H, middle, "load", shade, nothing(middle))
+        advance(step, x0 + step, nx - 2 * step, own, 8, "roll")
+    centre = advance(STEPS, x0 + H, nx - 2 * H, middle, 8, "load", shade, [nothing(ny - 2 * H)])[0]
     for i in range(5):
-        mid_acc[i] = carry[i]
+        mid_acc[i] = centre[i]
 
     for copy in sends:
         copy.wait_recv()
-    y_first, wide_rows = Y0 - H, ny + 2 * H
-    prepare(1, H, y_first, wide_rows, "load")
-    prepare(x0 + nx - 1, H + 1, y_first, wide_rows, "load")
-    edges = ((Y0 - H, 2 * H), (Y0 + ny - H, 2 * H))
-    for row, rows in edges:
-        prepare(x0, nx - 1, row, rows, "load")
+    edges = [(Y0 - H, 2 * H), (Y0 + ny - H, 2 * H)]
+    prepare(1, nx + 2 * H, edges, 24)
+    prepare(1, H, middle, H)
+    prepare(last, H + 1, middle, H + 1)
     for step in range(1, STEPS):
-        advance(step, x0 - H + step, H, y_first, wide_rows, "load")
-        for row, rows in edges:
-            advance(step, x0 + step, nx - 2 * step, row, rows, "load")
-        advance(step, x0 + nx - step, H, y_first, wide_rows, "load")
-    carry = advance(STEPS, x0, H, y_first, wide_rows, "load", shade, nothing(wide_rows))
+        advance(step, x0 - H + step, nx + 2 * H - 2 * step, edges, 28)
+        advance(step, x0 - H + step, H, middle, H)
+        advance(step, x0 + nx - step, H, middle, H)
+    left, right = advance(STEPS, x0, nx, edges, 16, "load", shade, [nothing(2 * H)] * 2)
+    front = advance(STEPS, x0, H, middle, H, "load", shade, [nothing(ny - 2 * H)])[0]
+    depth = front[0] + mid_acc[0]
+    centre = (depth, jnp.exp2(-depth)) + tuple(front[i] + front[1] * mid_acc[i] for i in (2, 3, 4))
+    centre = advance(STEPS, x0 + nx - H, H, middle, H, "load", shade, [centre])[0]
     for i in range(5):
-        acc[i] = carry[i]
-    for row, rows in edges:
-        carry = tuple(acc[i, row - y_first:row - y_first + rows] for i in range(5))
-        carry = advance(STEPS, x0 + H, nx - 2 * H, row, rows, "load", shade, carry)
-        for i in range(5):
-            acc[i, row - y_first:row - y_first + rows] = carry[i]
-    inner = slice(2 * H, 2 * H + middle)
-    front = acc[1, inner]
-    for i in (2, 3, 4):
-        acc[i, inner] = acc[i, inner] + front * mid_acc[i]
-    depth = acc[0, inner] + mid_acc[0]
-    acc[0, inner] = depth
-    acc[1, inner] = jnp.exp2(-depth)
-    carry = tuple(acc[i] for i in range(5))
-    carry = advance(STEPS, x0 + nx - H, H, y_first, wide_rows, "load", shade, carry)
-    for i in range(5):
-        acc[i] = carry[i]
+        acc[i, 0:2 * H] = left[i]
+        acc[i, 2 * H:ny] = centre[i]
+        acc[i, ny:ny + 2 * H] = right[i]
 
     store = pltpu.make_async_copy(c4.at[own_planes, own_rows], out, out_sem)
     store.start()

time: 40.5 us -> 34.1 us (0.84)
  Pallas kernels: 36 us -> 29.7 us
    pallas_call x1, Pallas kernels: 36 us -> 29.7 us  [on_device(): pl.pallas_call(functools.partial(kernel, nx, ny, nz, views, wides), out_s...]
where the time goes in v2:
time: 34.1 us; the launch traced here: 33.9 us
  Pallas kernels  29.7 us (87%)
  local copies, waits for them, and re-layouts  3.64 us (11%)
  between operations  0.64 us (2%)
    pallas_call x1, Pallas kernels, on_device(): pl.pallas_call(functools.partial(kernel, nx, ny, nz, views, wides), out_s...  29.7 us
    unnamed x2, local copies, waits for them, and re-layouts  3.64 us

profile of v2, /device:TPU:32, one launch (start us, length us, event | category | flops | bytes accessed | tf_op | source)
XLA Modules:
  0.0 33.9 jit_solution(14760596447465011211)
XLA Ops:
  0.6 29.7 %shard_map.59 = (f32[64,32,128]{2,1,0:T(8,128)}, f32[4,16,32]{2,1,0:T(8,128)}) custom-call(f32[64,32,128]{2,1,0:T(8,128)} %tracer.1, f32[3,64,32,128]{3,2,1,0:T(8,128)} %velocity.1, s32[64,32,128]{2,1,0:T(8,128)} %buildings.1, f32[64,32,128]{2,1,0:T(8,128)} %source.1), custom_call_target="tpu_custom_call" | custom-call | tf_op jit(solution)/shard_map/pallas_call | solution.py:264
  30.3 2.3 %copy.8 = f32[64,32,128]{2,1,0:T(8,128)} copy(f32[64,32,128]{2,1,0:T(8,128)} %get-tuple-element.8) | data formatting | bytes 2097152
  32.6 1.4 %copy.9 = f32[4,32,16]{1,2,0:T(8,128)} copy(f32[4,32,16]{1,2,0:T(8,128)} %bitcast.1) | data formatting | bytes 16384

commit v3 on v2

--- a/solution.py
+++ b/solution.py
@@ -51,30 +51,34 @@
     out, picture,
     t_raw, v_raw, b_raw, s_raw, wx, wy, wz, src, c0, c1, c2, c3, c4,
     acc, mid_acc, part, pieces,
-    local_sem, out_sem, send_sem, recv_sem, piece_send, piece_recv,
+    local_sem, out_sem, known_sem, send_sem, recv_sem, piece_send, piece_recv,
 ):
     my_view, my_wide = lax.axis_index("view"), lax.axis_index("wide")
 
     def device(dv, dw):
         return (lax.rem(my_view + dv + views, views), lax.rem(my_wide + dw + wides, wides))
 
-    neighbours = [(dv, dw) for dv in (0, 1, -1) for dw in (0, 1, -1) if (dv, dw) != (0, 0)]
-    far = [(dv, 0) for dv in range(2, views - 1)]
+    near = [(1, 0), (-1, 0), (0, 1), (0, -1)]
+    corners = [(dv, dw) for dv in (1, -1) for dw in (1, -1)]
 
     own_planes, own_rows = pl.ds(H + 1, nx), pl.ds(Y0, ny)
     loads = [
-        pltpu.make_async_copy(buildings, b_raw.at[own_planes, own_rows], local_sem.at[0]),
-        pltpu.make_async_copy(velocity, v_raw.at[:, own_planes, own_rows], local_sem.at[1]),
-        pltpu.make_async_copy(tracer, t_raw.at[own_planes, own_rows], local_sem.at[2]),
+        pltpu.make_async_copy(buildings, b_raw, local_sem.at[0]),
+        pltpu.make_async_copy(tracer, t_raw, local_sem.at[1]),
+        pltpu.make_async_copy(velocity, v_raw.at[:, own_planes, own_rows], local_sem.at[2]),
         pltpu.make_async_copy(source, s_raw.at[own_planes, own_rows], local_sem.at[3]),
     ]
     for load in loads:
         load.start()
 
     barrier = pltpu.get_barrier_semaphore()
-    for dv, dw in neighbours + far:
+    for dv, dw in near:
         pl.semaphore_signal(barrier, inc=1, device_id=device(dv, dw), device_id_type=MESH)
-    pl.semaphore_wait(barrier, len(neighbours) + len(far))
+    pl.semaphore_wait(barrier, len(near))
+
+    def tell(ring, sides):
+        for dv, dw in sides:
+            pl.semaphore_signal(known_sem.at[ring], inc=1, device_id=device(dv, dw), device_id_type=MESH)
 
     sends = []
 
@@ -94,10 +98,7 @@
         copy.start()
         sends.append(copy)
 
-    for dv, dw in sorted(neighbours, key=lambda n: -abs(n[0]) - 2 * abs(n[0] * n[1])):
-        corner = dv != 0 and dw != 0
-        send(buildings, b_raw, dv, dw, H - 1 if corner else H)
-        send(tracer, t_raw, dv, dw, H - 1 if corner else H)
+    def send_inputs(dv, dw):
         if (dv, dw) == (1, 0):
             send(velocity, v_raw, dv, dw, H, pl.ds(0, 1))
             send(velocity, v_raw, dv, dw, H - 1, pl.ds(1, 2))
@@ -107,28 +108,31 @@
             send(velocity, v_raw, dv, dw, H - 1, pl.ds(2, 1))
         else:
             send(velocity, v_raw, dv, dw, H - 1, pl.ds(0, 3))
-        send(source, s_raw, dv, dw, H - 2 if corner else H - 1)
+        send(source, s_raw, dv, dw, H - 2 if dv and dw else H - 1)
+
+    def send_tracer(dv, dw):
+        block = c0.at[own_planes, own_rows]
+        send(block, c0, dv, dw, H - 1 if dv and dw else H)
 
     levels = (c0, c1, c2, c3, c4)
     below_top = lax.broadcasted_iota(jnp.int32, (1, nz), 1) < nz - 1
 
     def prepare(first, count, windows, unroll, shift="load"):
-        def body(p, built):
-            return tuple(cells(p, row, rows, b_here) for (row, rows), b_here in zip(windows, built))
-
-        def cells(p, row, rows, b_here):
+        def body(p, here_cs):
+            return tuple(cells(p, row, rows, here_c) for (row, rows), here_c in zip(windows, here_cs))
+
+        def cells(p, row, rows, here_c):
             here = pl.ds(row, rows)
-            b_next = b_raw[p + 1, here, :]
-            b_up = pltpu.roll(b_here, rows - 1, 0) if shift == "roll" else b_raw[p, pl.ds(row + 1, rows), :]
-            open_here = b_here == 0
-            wx[p, here, :] = jnp.where((b_here | b_next) == 0, v_raw[0, p, here, :], 0.0)
-            wy[p, here, :] = jnp.where((b_here | b_up) == 0, v_raw[1, p, here, :], 0.0)
+            next_c = c0[p + 1, here, :]
+            up_c = pltpu.roll(here_c, rows - 1, 0) if shift == "roll" else c0[p, pl.ds(row + 1, rows), :]
+            open_here = here_c > 0.0
+            wx[p, here, :] = jnp.where(jnp.minimum(here_c, next_c) > 0.0, v_raw[0, p, here, :], 0.0)
+            wy[p, here, :] = jnp.where(jnp.minimum(here_c, up_c) > 0.0, v_raw[1, p, here, :], 0.0)
             wz[p, here, :] = jnp.where(open_here & below_top, v_raw[2, p, here, :], 0.0)
             src[p, here, :] = jnp.where(open_here, s_raw[p, here, :], 0.0)
-            c0[p, here, :] = jnp.where(open_here, t_raw[p, here, :], 0.0)
-            return b_next
-
-        sweep(first, count, unroll, body, tuple(b_raw[first, pl.ds(row, rows), :] for row, rows in windows))
+            return next_c
+
+        sweep(first, count, unroll, body, tuple(c0[first, pl.ds(row, rows), :] for row, rows in windows))
 
     def advance(step, first, count, windows, unroll, shift="load", shade=None, carries=None):
         old, new = levels[step - 1], levels[step]
@@ -153,7 +157,7 @@
             value = here_c + src[p, here, :] - (flux_x - flux_low) - (flux_y - flux_y_low) - (flux_z - flux_z_low)
             new[p, here, :] = value
             if shade is not None:
-                carry = shade(value, b_raw[p, here, :], carry)
+                carry = shade(value, c0[p, here, :], carry)
             return next_c, flux_x, carry
 
         states = []
@@ -166,9 +170,9 @@
 
     scale = LOG2E / (nx * views)
 
-    def shade(value, built, carry):
+    def shade(value, start, carry):
         depth, through, red, green, blue = carry
-        wall = built != 0
+        wall = start <= 0.0
         depth = depth + jnp.where(wall, 4.0, value) * scale
         after = jnp.exp2(-depth)
         weight = through - after
@@ -184,13 +188,36 @@
 
     x0 = H + 1
     last = x0 + nx - 1
-    for load in loads:
+    own, middle = [(Y0, ny)], [(Y0 + H, ny - 2 * H)]
+    for side in near:
+        send_inputs(*side)
+    tell(0, near)
+    for load in loads[:2]:
         load.wait()
-    own, middle = [(Y0, ny)], [(Y0 + H, ny - 2 * H)]
+
+    def mask_plane(p, carry):
+        c0[p, own_rows, :] = jnp.where(b_raw[p - x0] == 0, t_raw[p - x0], 0.0)
+        return carry
+
+    sweep(x0, nx, 16, mask_plane, 0)
+    for side in near:
+        send_tracer(*side)
+    pl.semaphore_wait(known_sem.at[0], len(near))
+    if views // 2 > 2:
+        tell(1, near[:2])
+    for side in corners:
+        send_inputs(*side)
+        send_tracer(*side)
+    for load in loads[2:]:
+        load.wait()
     prepare(x0, nx - 1, own, 8, "roll")
-    c0[last, own_rows, :] = jnp.where(b_raw[last, own_rows, :] == 0, t_raw[last, own_rows, :], 0.0)
     for step in range(1, STEPS):
         advance(step, x0 + step, nx - 2 * step, own, 8, "roll")
+        ring = step
+        if ring < views // 2 - 1:
+            pl.semaphore_wait(known_sem.at[ring], 2)
+            if ring < views // 2 - 2:
+                tell(ring + 1, near[:2])
     centre = advance(STEPS, x0 + H, nx - 2 * H, middle, 8, "load", shade, [nothing(ny - 2 * H)])[0]
     for i in range(5):
         mid_acc[i] = centre[i]
@@ -270,9 +297,9 @@
         in_specs=[pl.BlockSpec(memory_space=pltpu.HBM)] * 4,
         out_specs=(pl.BlockSpec(memory_space=pltpu.HBM), pl.BlockSpec(memory_space=pltpu.VMEM)),
         scratch_shapes=[
-            buffer,
+            pltpu.VMEM((nx, ny, nz), jnp.float32),
             pltpu.VMEM((3,) + field, jnp.float32),
-            pltpu.VMEM(field, jnp.int32),
+            pltpu.VMEM((nx, ny, nz), jnp.int32),
         ]
         + [buffer] * 10
         + [
@@ -282,13 +309,14 @@
             pltpu.VMEM((views, nz // views, 4 * ny), jnp.float32),
             pltpu.SemaphoreType.DMA((4,)),
             pltpu.SemaphoreType.DMA,
+            pltpu.SemaphoreType.REGULAR((views // 2 - 1,)),
             pltpu.SemaphoreType.DMA((n_sends,)),
             pltpu.SemaphoreType.DMA((n_sends,)),
             pltpu.SemaphoreType.DMA((views - 1,)),
             pltpu.SemaphoreType.DMA((views - 1,)),
         ],
         compiler_params=pltpu.CompilerParams(
-            collective_id=0, has_side_effects=True, vmem_limit_bytes=60 * 1024 * 1024
+            collective_id=0, has_side_effects=True, vmem_limit_bytes=52 * 1024 * 1024
         ),
     )(tracer, velocity, buildings, source)
     return tracer_next, jnp.swapaxes(picture, 1, 2)

time: 34.1 us -> 29.2 us (0.86)
  Pallas kernels: 29.7 us -> 26.9 us
  local copies, waits for them, and re-layouts: 3.64 us -> 1.59 us
    pallas_call x1, Pallas kernels: 29.7 us -> 26.9 us  [on_device(): pl.pallas_call(functools.partial(kernel, nx, ny, nz, views, wides), out_s...]
    unnamed x2, local copies, waits for them, and re-layouts: 3.64 us -> 1.59 us
where the time goes in v3:
time: 29.2 us; the launch traced here: 29.1 us
  Pallas kernels  26.9 us (92%)
  local copies, waits for them, and re-layouts  1.59 us (5%)
  between operations  0.64 us (2%)
    pallas_call x1, Pallas kernels, on_device(): pl.pallas_call(functools.partial(kernel, nx, ny, nz, views, wides), out_s...  26.9 us
    unnamed x2, local copies, waits for them, and re-layouts  1.59 us

profile of v3, /device:TPU:32, one launch (start us, length us, event | category | flops | bytes accessed | tf_op | source)
XLA Modules:
  0.0 29.1 jit_solution(18013692663396203715)
XLA Ops:
  0.6 26.9 %shard_map.59 = (f32[64,32,128]{2,1,0:T(8,128)S(1)}, f32[4,16,32]{2,1,0:T(8,128)S(1)}) custom-call(f32[64,32,128]{2,1,0:T(8,128)} %tracer.1, f32[3,64,32,128]{3,2,1,0:T(8,128)} %velocity.1, s32[64,32,128]{2,1,0:T(8,128)} %buildings.1, f32[64,32,128]{2,1,0:T(8,128)} %source.1), custom_call_target="tpu_custom_call" | custom-call | tf_op jit(solution)/shard_map/pallas_call | solution.py:291
  27.5 1.0 %copy.8 = f32[64,32,128]{2,1,0:T(8,128)} copy(f32[64,32,128]{2,1,0:T(8,128)S(1)} %get-tuple-element.8) | data formatting | bytes 2097152
  28.5 0.6 %copy.9 = f32[4,32,16]{1,2,0:T(8,128)} copy(f32[4,32,16]{1,2,0:T(8,128)S(1)} %bitcast.1) | data formatting | bytes 16384

commit v4 on v3

--- a/solution.py
+++ b/solution.py
@@ -46,7 +46,7 @@
 
 
 def kernel(
-    nx, ny, nz, views, wides,
+    nx, ny, nz, views, wides, split,
     tracer, velocity, buildings, source,
     out, picture,
     t_raw, v_raw, b_raw, s_raw, wx, wy, wz, src, c0, c1, c2, c3, c4,
@@ -82,8 +82,11 @@
 
     sends = []
 
-    def send(ref, buffer, dv, dw, depth, pick=None):
+    def send(ref, buffer, dv, dw, depth, pick=None, part=None):
         xs, xd, xn = face_range(dv, nx, depth)
+        if part is not None:
+            xs, xn = ((0, split), (split, nx - split))[part]
+            xd = xs
         ys, yd, yn = face_range(dw, ny, depth)
         here = (pl.ds(xs, xn), pl.ds(ys, yn))
         there = (pl.ds(xd + H + 1, xn), pl.ds(yd + Y0, yn))
@@ -96,23 +99,23 @@
             device_id=device(dv, dw), device_id_type=MESH,
         )
         copy.start()
-        sends.append(copy)
-
-    def send_inputs(dv, dw):
+        sends.append((copy, part))
+
+    def send_inputs(dv, dw, part=None):
         if (dv, dw) == (1, 0):
-            send(velocity, v_raw, dv, dw, H, pl.ds(0, 1))
-            send(velocity, v_raw, dv, dw, H - 1, pl.ds(1, 2))
+            send(velocity, v_raw, dv, dw, H, pl.ds(0, 1), part)
+            send(velocity, v_raw, dv, dw, H - 1, pl.ds(1, 2), part)
         elif (dv, dw) == (0, 1):
-            send(velocity, v_raw, dv, dw, H, pl.ds(1, 1))
-            send(velocity, v_raw, dv, dw, H - 1, pl.ds(0, 1))
-            send(velocity, v_raw, dv, dw, H - 1, pl.ds(2, 1))
+            send(velocity, v_raw, dv, dw, H, pl.ds(1, 1), part)
+            send(velocity, v_raw, dv, dw, H - 1, pl.ds(0, 1), part)
+            send(velocity, v_raw, dv, dw, H - 1, pl.ds(2, 1), part)
         else:
-            send(velocity, v_raw, dv, dw, H - 1, pl.ds(0, 3))
-        send(source, s_raw, dv, dw, H - 2 if dv and dw else H - 1)
-
-    def send_tracer(dv, dw):
+            send(velocity, v_raw, dv, dw, H - 1, pl.ds(0, 3), part)
+        send(source, s_raw, dv, dw, H - 2 if dv and dw else H - 1, None, part)
+
+    def send_tracer(dv, dw, part=None):
         block = c0.at[own_planes, own_rows]
-        send(block, c0, dv, dw, H - 1 if dv and dw else H)
+        send(block, c0, dv, dw, H - 1 if dv and dw else H, None, part)
 
     levels = (c0, c1, c2, c3, c4)
     below_top = lax.broadcasted_iota(jnp.int32, (1, nz), 1) < nz - 1
@@ -182,14 +185,21 @@
         blue = blue + weight * jnp.where(wall, 0.45, 0.2 + 0.6 * (shading * shading))
         return depth, after, red, green, blue
 
+    def behind(front, back):
+        depth = front[0] + back[0]
+        return (depth, jnp.exp2(-depth)) + tuple(front[i] + front[1] * back[i] for i in (2, 3, 4))
+
     def nothing(rows):
         zero = jnp.zeros((rows, nz), jnp.float32)
         return zero, jnp.ones((rows, nz), jnp.float32), zero, zero, zero
 
     x0 = H + 1
     last = x0 + nx - 1
-    own, middle = [(Y0, ny)], [(Y0 + H, ny - 2 * H)]
-    for side in near:
+    own, middle, wide = [(Y0, ny)], [(Y0 + H, ny - 2 * H)], [(Y0 - H, ny + 2 * H)]
+    along, across = near[:2], near[2:]
+    for side in across:
+        send_inputs(*side, 0)
+    for side in along:
         send_inputs(*side)
     tell(0, near)
     for load in loads[:2]:
@@ -200,8 +210,14 @@
         return carry
 
     sweep(x0, nx, 16, mask_plane, 0)
-    for side in near:
+    for side in across:
+        send_tracer(*side, 0)
+    early = [copy for copy, half in sends if half == 0]
+    for side in along:
         send_tracer(*side)
+    for side in across:
+        send_inputs(*side, 1)
+        send_tracer(*side, 1)
     pl.semaphore_wait(known_sem.at[0], len(near))
     if views // 2 > 2:
         tell(1, near[:2])
@@ -222,20 +238,28 @@
     for i in range(5):
         mid_acc[i] = centre[i]
 
-    for copy in sends:
+    for copy in early:
         copy.wait_recv()
     edges = [(Y0 - H, 2 * H), (Y0 + ny - H, 2 * H)]
-    prepare(1, nx + 2 * H, edges, 24)
-    prepare(1, H, middle, H)
+    prepare(x0, split - 1, edges, 20)
+    for step in range(1, STEPS):
+        advance(step, x0 + step, split - 2 * step, edges, 20)
+    early_edges = advance(STEPS, x0 + H, split - 2 * H, edges, 16, "load", shade, [nothing(2 * H)] * 2)
+    for copy, half in sends:
+        if half != 0:
+            copy.wait_recv()
+    prepare(1, H, wide, H)
+    prepare(x0 + split - 1, nx - split + H + 1, edges, 28)
     prepare(last, H + 1, middle, H + 1)
     for step in range(1, STEPS):
-        advance(step, x0 - H + step, nx + 2 * H - 2 * step, edges, 28)
-        advance(step, x0 - H + step, H, middle, H)
+        advance(step, x0 - H + step, H, wide, H)
+        advance(step, x0 + split - step, nx - split + H, edges, 28)
         advance(step, x0 + nx - step, H, middle, H)
-    left, right = advance(STEPS, x0, nx, edges, 16, "load", shade, [nothing(2 * H)] * 2)
+    front_edges = advance(STEPS, x0, H, edges, H, "load", shade, [nothing(2 * H)] * 2)
+    edge_carries = [behind(f, b) for f, b in zip(front_edges, early_edges)]
+    left, right = advance(STEPS, x0 + split - H, nx - split + H, edges, 18, "load", shade, edge_carries)
     front = advance(STEPS, x0, H, middle, H, "load", shade, [nothing(ny - 2 * H)])[0]
-    depth = front[0] + mid_acc[0]
-    centre = (depth, jnp.exp2(-depth)) + tuple(front[i] + front[1] * mid_acc[i] for i in (2, 3, 4))
+    centre = behind(front, [mid_acc[i] for i in range(5)])
     centre = advance(STEPS, x0 + nx - H, H, middle, H, "load", shade, [centre])[0]
     for i in range(5):
         acc[i, 0:2 * H] = left[i]
@@ -249,7 +273,7 @@
     part[...] = stacked.T
     share = nz // views
     copies = []
-    for hop in range(1, views):
+    for hop in sorted(range(1, views), key=lambda hop: -min(hop, views - hop)):
         target = lax.rem(my_view + hop, views)
         copy = pltpu.make_async_remote_copy(
             src_ref=part.at[pl.ds(pl.multiple_of(target * share, share), share)],
@@ -277,9 +301,23 @@
     for i in range(4):
         picture[i] = pixels[:, i * ny:(i + 1) * ny]
 
-    for copy in sends + copies:
+    for copy in [copy for copy, half in sends] + copies:
         copy.wait_send()
     store.wait()
+
+
+def finish(tracer_next, picture, tracer_out, picture_out, sem):
+    planes = tracer_next.shape[0]
+    parts = 8
+    each = planes // parts
+    copies = [pltpu.make_async_copy(picture, picture_out, sem.at[parts])]
+    for i in range(parts):
+        here = pl.ds(i * each, each)
+        copies.append(pltpu.make_async_copy(tracer_next.at[here], tracer_out.at[here], sem.at[i]))
+    for copy in copies:
+        copy.start()
+    for copy in copies:
+        copy.wait()
 
 
 def on_device(tracer, velocity, buildings, source):
@@ -289,7 +327,7 @@
     buffer = pltpu.VMEM(field, jnp.float32)
     n_sends = 40
     tracer_next, picture = pl.pallas_call(
-        functools.partial(kernel, nx, ny, nz, views, wides),
+        functools.partial(kernel, nx, ny, nz, views, wides, nx * 5 // 8),
         out_shape=(
             jax.ShapeDtypeStruct((nx, ny, nz), jnp.float32),
             jax.ShapeDtypeStruct((4, nz // views, ny), jnp.float32),
@@ -319,6 +357,17 @@
             collective_id=0, has_side_effects=True, vmem_limit_bytes=52 * 1024 * 1024
         ),
     )(tracer, velocity, buildings, source)
+    tracer_next, picture = pl.pallas_call(
+        finish,
+        out_shape=(
+            jax.ShapeDtypeStruct(tracer_next.shape, jnp.float32),
+            jax.ShapeDtypeStruct(picture.shape, jnp.float32),
+        ),
+        in_specs=[pl.BlockSpec(memory_space=pl.ANY)] * 2,
+        out_specs=(pl.BlockSpec(memory_space=pltpu.HBM),) * 2,
+        scratch_shapes=[pltpu.SemaphoreType.DMA((9,))],
+        compiler_params=pltpu.CompilerParams(vmem_limit_bytes=1024 * 1024),
+    )(tracer_next, picture)
     return tracer_next, jnp.swapaxes(picture, 1, 2)
 
 

time: 29.2 us -> 27.4 us (0.938)
  local copies, waits for them, and re-layouts: 1.59 us -> 0 us
  Pallas kernels: 26.9 us -> 26.6 us
    unnamed x2 -> x0, local copies, waits for them, and re-layouts: 1.59 us -> none
    pallas_call x1 -> x2, Pallas kernels: 26.9 us -> 26.6 us  [the longest x1 25.5 us: on_device(): pl.pallas_call(functools.partial(kernel, nx, ny, nz, views, wides, nx * 5...]
where the time goes in v4:
time: 27.4 us; the launch traced here: 27.2 us
  Pallas kernels  26.6 us (97%)
  between operations  0.64 us (2%)
    pallas_call x1, Pallas kernels, on_device(): pl.pallas_call(functools.partial(kernel, nx, ny, nz, views, wides, nx * 5...  25.5 us
    pallas_call x1, Pallas kernels, on_device(): pl.pallas_call(finish, out_shape=(jax.ShapeDtypeStruct(tracer_next.shape,...  1.05 us

profile of v4, /device:TPU:32, one launch (start us, length us, event | category | flops | bytes accessed | tf_op | source)
XLA Modules:
  0.0 27.2 jit_solution(13247451590939954591)
XLA Ops:
  0.6 25.5 %shard_map.59 = (f32[64,32,128]{2,1,0:T(8,128)S(1)}, f32[4,16,32]{2,1,0:T(8,128)S(1)}) custom-call(f32[64,32,128]{2,1,0:T(8,128)} %tracer.1, f32[3,64,32,128]{3,2,1,0:T(8,128)} %velocity.1, s32[64,32,128]{2,1,0:T(8,128)} %buildings.1, f32[64,32,128]{2,1,0:T(8,128)} %source.1), custom_call_target="tpu_custom_call" | custom-call | tf_op jit(solution)/shard_map/pallas_call | solution.py:329
  26.2 1.0 %shard_map.60 = (f32[64,32,128]{2,1,0:T(8,128)}, f32[4,16,32]{2,1,0:T(8,128)}) custom-call(f32[64,32,128]{2,1,0:T(8,128)S(1)} %get-tuple-element.6.tracer_next, f32[4,16,32]{2,1,0:T(8,128)S(1)} %get-tuple-element.7.picture), custom_call_target="tpu_custom_call" | custom-call | tf_op jit(solution)/shard_map/pallas_call | solution.py:360

commit v5 on v4

--- a/solution.py
+++ b/solution.py
@@ -226,9 +226,9 @@
         send_tracer(*side)
     for load in loads[2:]:
         load.wait()
-    prepare(x0, nx - 1, own, 8, "roll")
+    prepare(x0, nx - 1, own, 16, "roll")
     for step in range(1, STEPS):
-        advance(step, x0 + step, nx - 2 * step, own, 8, "roll")
+        advance(step, x0 + step, nx - 2 * step, own, 16, "roll")
         ring = step
         if ring < views // 2 - 1:
             pl.semaphore_wait(known_sem.at[ring], 2)

time: 27.4 us -> 27.1 us (0.989)
  no operation moved by 1% of the time
where the time goes in v5:
time: 27.1 us; the launch traced here: 27 us
  Pallas kernels  26.4 us (97%)
  between operations  0.64 us (2%)
    pallas_call x1, Pallas kernels, on_device(): pl.pallas_call(functools.partial(kernel, nx, ny, nz, views, wides, nx * 5...  25.3 us
    pallas_call x1, Pallas kernels, on_device(): pl.pallas_call(finish, out_shape=(jax.ShapeDtypeStruct(tracer_next.shape,...  1.05 us

profile of v5, /device:TPU:32, one launch (start us, length us, event | category | flops | bytes accessed | tf_op | source)
XLA Modules:
  0.0 27.0 jit_solution(14407040307330300966)
XLA Ops:
  0.6 25.3 %shard_map.59 = (f32[64,32,128]{2,1,0:T(8,128)S(1)}, f32[4,16,32]{2,1,0:T(8,128)S(1)}) custom-call(f32[64,32,128]{2,1,0:T(8,128)} %tracer.1, f32[3,64,32,128]{3,2,1,0:T(8,128)} %velocity.1, s32[64,32,128]{2,1,0:T(8,128)} %buildings.1, f32[64,32,128]{2,1,0:T(8,128)} %source.1), custom_call_target="tpu_custom_call" | custom-call | tf_op jit(solution)/shard_map/pallas_call | solution.py:329
  26.0 1.0 %shard_map.60 = (f32[64,32,128]{2,1,0:T(8,128)}, f32[4,16,32]{2,1,0:T(8,128)}) custom-call(f32[64,32,128]{2,1,0:T(8,128)S(1)} %get-tuple-element.6.tracer_next, f32[4,16,32]{2,1,0:T(8,128)S(1)} %get-tuple-element.7.picture), custom_call_target="tpu_custom_call" | custom-call | tf_op jit(solution)/shard_map/pallas_call | solution.py:360

commit v6 on v5

--- a/solution.py
+++ b/solution.py
@@ -218,15 +218,15 @@
     for side in across:
         send_inputs(*side, 1)
         send_tracer(*side, 1)
+    for load in loads[2:]:
+        load.wait()
+    prepare(x0, nx - 1, own, 16, "roll")
     pl.semaphore_wait(known_sem.at[0], len(near))
     if views // 2 > 2:
         tell(1, near[:2])
     for side in corners:
         send_inputs(*side)
         send_tracer(*side)
-    for load in loads[2:]:
-        load.wait()
-    prepare(x0, nx - 1, own, 16, "roll")
     for step in range(1, STEPS):
         advance(step, x0 + step, nx - 2 * step, own, 16, "roll")
         ring = step

time: 27.1 us -> 27.1 us (level)
  no operation moved by 1% of the time
where the time goes in v6:
time: 27.1 us; the launch traced here: 27 us
  Pallas kernels  26.4 us (97%)
  between operations  0.64 us (2%)
    pallas_call x1, Pallas kernels, on_device(): pl.pallas_call(functools.partial(kernel, nx, ny, nz, views, wides, nx * 5...  25.3 us
    pallas_call x1, Pallas kernels, on_device(): pl.pallas_call(finish, out_shape=(jax.ShapeDtypeStruct(tracer_next.shape,...  1.05 us

profile of v6, /device:TPU:32, one launch (start us, length us, event | category | flops | bytes accessed | tf_op | source)
XLA Modules:
  0.0 27.0 jit_solution(17718976541605751550)
XLA Ops:
  0.6 25.3 %shard_map.59 = (f32[64,32,128]{2,1,0:T(8,128)S(1)}, f32[4,16,32]{2,1,0:T(8,128)S(1)}) custom-call(f32[64,32,128]{2,1,0:T(8,128)} %tracer.1, f32[3,64,32,128]{3,2,1,0:T(8,128)} %velocity.1, s32[64,32,128]{2,1,0:T(8,128)} %buildings.1, f32[64,32,128]{2,1,0:T(8,128)} %source.1), custom_call_target="tpu_custom_call" | custom-call | tf_op jit(solution)/shard_map/pallas_call | solution.py:329
  26.0 1.0 %shard_map.60 = (f32[64,32,128]{2,1,0:T(8,128)}, f32[4,16,32]{2,1,0:T(8,128)}) custom-call(f32[64,32,128]{2,1,0:T(8,128)S(1)} %get-tuple-element.6.tracer_next, f32[4,16,32]{2,1,0:T(8,128)S(1)} %get-tuple-element.7.picture), custom_call_target="tpu_custom_call" | custom-call | tf_op jit(solution)/shard_map/pallas_call | solution.py:360
